TPU v7x, 128 devices: a whole 4x4x4 slice. The times are simulated.
128 devices in a mesh: tm: 8 (over x, core), seq: 16 (over z, y).
Axes of the slice: x: 4, y: 4, z: 4, core: 2. Of those that a mesh axis runs over, the one named last changes fastest.
Arguments:
- hidden: bfloat16 [8, 2, 2048, 2432], P('tm', None, 'seq'), may hold values from -6 to 6
- text_states: bfloat16 [8, 2, 256, 2560], P('tm', None, 'seq'), may hold values from -6 to 6
- text_lengths: int32 [2], replicated, may hold values from 1 to 256
- plan_index: int32 [8], P('tm'), may hold values from 0 to 27, as said below
- modulation: float32 [8, 5, 2432], P('tm'), may hold values from -3 to 3
- query_key_value_weight: bfloat16 [2432, 3840], replicated, may hold values from -0.125 to 0.125
- query_gain: float32 [64], replicated, may hold values from 0.5 to 7
- key_gain: float32 [64], replicated, may hold values from 0.5 to 7
- attention_output_weight: bfloat16 [1280, 2432], replicated, may hold values from -0.15625 to 0.15625
- latent_output_weight: bfloat16 [2432, 64], replicated, may hold values from -0.125 to 0.125
- anchor: float32 [2048, 64], P('seq'), may hold values from -6 to 6
Outputs:
- velocity: float32 [8, 2048, 64], P('tm', 'seq')
- latents: float32 [8, 2048, 64], P('tm', 'seq')
Inputs may be any that keep to these rules, and one draw needn't show every extreme that they name: `plan_index`: strictly increasing along the window; the last window step is at plan position 27.
All inputs are finite; a program needn't handle non-finite values.
Results may differ from a plain program's by a relative error of at most 0.0075.
The roundings to bfloat16 on the way count: a program that leaves them out, or rounds other values in their place, can miss the bound.
Values may be sent and summed in bfloat16 or wider, within the bound.
A program may use at most 192 MiB of HBM per device.

v0:
```python
import math

import jax
import jax.numpy as jnp
from jax import lax
from jax.sharding import PartitionSpec as P

NSTEPS = 28


EPSILON = 1e-06
NEG_LARGE = -1e30
GUIDANCE = 3.5
TIME_SHIFT = 3.0


def from_behind(block, axis, distance):
    devices = range(lax.axis_size(axis))
    route = [(i - distance, i) for i in devices if i - distance in devices]
    return lax.ppermute(block, axis, route)


def carried_in(value, axis, join, neutral):
    place = lax.axis_index(axis)
    gathered = lax.all_gather(value.astype(jnp.bfloat16), axis)
    state = jnp.zeros_like(value) + jnp.asarray(neutral, value.dtype)

    def one(lap, state):
        return join(state, lax.dynamic_index_in_dim(gathered, lap, 0, False).astype(value.dtype))

    return lax.fori_loop(0, place, one, state)


def layer_norm(inputs):
    values = inputs.astype(jnp.float32)
    center = jnp.mean(values, axis=-1, keepdims=True)
    spread = jnp.mean(jnp.square(values - center), axis=-1, keepdims=True)
    return (values - center) / jnp.sqrt(spread + EPSILON)


def head_norm(inputs, gain_vector, head_size):
    shaped = inputs.astype(jnp.float32).reshape(inputs.shape[:-1] + (-1, head_size))
    rms_value = jnp.sqrt(jnp.mean(jnp.square(shaped), axis=-1, keepdims=True) + EPSILON)
    return (shaped / rms_value * gain_vector).astype(jnp.bfloat16)


def sigma_of(index_values):
    fraction = 1.0 - index_values.astype(jnp.float32) / NSTEPS
    return TIME_SHIFT * fraction / (1.0 + (TIME_SHIFT - 1.0) * fraction)


def attend(running, key_rows, allowed, query, scale_factor):
    maxima, denominator, numerator = running
    heads = query.shape[2]
    head_size = query.shape[3]
    inner = heads * head_size
    row_count = key_rows.shape[1]
    key_part = key_rows[:, :, :inner].reshape(2, row_count, heads, head_size)
    value_part = key_rows[:, :, inner:].reshape(2, row_count, heads, head_size)
    scores = (
        jnp.einsum("bqhd,bkhd->bhqk", query, key_part, preferred_element_type=jnp.float32)
        * scale_factor
    )
    keep_mask = allowed[:, None, None, :]
    masked = jnp.where(keep_mask, scores, NEG_LARGE)
    new_max = jnp.maximum(maxima, jnp.max(masked, axis=-1))
    factor = jnp.exp(maxima - new_max)
    expon = jnp.where(keep_mask, jnp.exp(masked - new_max[..., None]), 0.0)
    denominator = denominator * factor + jnp.sum(expon, axis=-1)
    numerator = numerator * factor[..., None] + jnp.einsum(
        "bhqk,bkhd->bhqd",
        expon.astype(jnp.bfloat16),
        value_part,
        preferred_element_type=jnp.float32,
    )
    return (new_max, denominator, numerator)


def add_terms(earlier, later):
    return earlier + later


def on_device(
    hidden,
    text_states,
    text_lengths,
    plan_index,
    modulation,
    query_key_value_weight,
    query_gain,
    key_gain,
    attention_output_weight,
    latent_output_weight,
    anchor,
):
    head_size = query_gain.shape[0]
    inner = attention_output_weight.shape[0]
    heads = inner // head_size
    image_rows = hidden.shape[2]
    text_rows = text_states.shape[2]
    scale_factor = 1.0 / math.sqrt(head_size)
    rows_mod = modulation[0]
    normalized_states = (layer_norm(hidden[0]) * (1.0 + rows_mod[1]) + rows_mod[0]).astype(
        jnp.bfloat16
    )
    projected = jnp.einsum(
        "kvx,xh->kvh", normalized_states, query_key_value_weight, preferred_element_type=jnp.float32
    ).astype(jnp.bfloat16)
    query = head_norm(projected[:, :, :inner], query_gain, head_size)
    image_keys = head_norm(projected[:, :, inner : 2 * inner], key_gain, head_size).reshape(
        2, image_rows, inner
    )
    image_local = jnp.concatenate([image_keys, projected[:, :, 2 * inner :]], axis=2)
    text_keys = head_norm(text_states[0][:, :, :inner], key_gain, head_size).reshape(
        2, text_rows, inner
    )
    text_local = jnp.concatenate([text_keys, text_states[0][:, :, inner:]], axis=2)
    initial = (
        jnp.full((2, heads, image_rows), NEG_LARGE, jnp.float32),
        jnp.zeros((2, heads, image_rows), jnp.float32),
        jnp.zeros((2, heads, image_rows, head_size), jnp.float32),
    )
    text_all = lax.all_gather(text_local, "seq", axis=1, tiled=True)
    text_allowed = jnp.arange(text_all.shape[1], dtype=jnp.int32)[None, :] < text_lengths[:, None]
    running = attend(initial, text_all, text_allowed, query, scale_factor)
    key_rows = lax.all_gather(image_local, "seq", axis=1, tiled=True)
    allowed = jnp.ones((2, key_rows.shape[1]), dtype=bool)
    running = attend(running, key_rows, allowed, query, scale_factor)
    maxima, denominator, numerator = running
    projected_attention = (numerator / denominator[..., None]).astype(jnp.bfloat16)
    projected_attention = projected_attention.transpose(0, 2, 1, 3).reshape(2, image_rows, inner)
    attention_output = jnp.einsum(
        "ixw,wn->ixn",
        projected_attention,
        attention_output_weight,
        preferred_element_type=jnp.float32,
    )
    second = hidden[0].astype(jnp.float32) + rows_mod[2] * attention_output
    final_latent_output = (layer_norm(second) * (1.0 + rows_mod[4]) + rows_mod[3]).astype(
        jnp.bfloat16
    )
    branch_velocity = jnp.einsum(
        "gof,fn->gon", final_latent_output, latent_output_weight, preferred_element_type=jnp.float32
    )
    velocity = branch_velocity[0] + GUIDANCE * (branch_velocity[1] - branch_velocity[0])
    next_index = from_behind(plan_index, "tm", -1)
    is_last = lax.axis_index("tm") == lax.axis_size("tm") - 1
    following = jnp.where(is_last, jnp.int32(NSTEPS), next_index)
    step_size = sigma_of(following) - sigma_of(plan_index)
    drift = step_size[0] * velocity
    earlier = carried_in(drift, "tm", add_terms, jnp.zeros_like(drift))
    summed = earlier + drift
    latents = anchor + summed
    return (velocity[None], latents[None])


def solution(mesh):
    in_specs = (
        P("tm", None, "seq", None),
        P("tm", None, "seq", None),
        P(),
        P("tm"),
        P("tm", None, None),
        P(),
        P(),
        P(),
        P(),
        P(),
        P("seq", None),
    )
    out_specs = (P("tm", "seq", None), P("tm", "seq", None))
    return jax.shard_map(
        on_device, mesh=mesh, in_specs=in_specs, out_specs=out_specs, check_vma=False
    )
```

profile of v0, /device:TPU:15, one launch (start us, length us, event | category | flops | bytes accessed | tf_op | source)
XLA Modules:
  0.0 328.9 jit_solution(10547081349934933478)
XLA Ops:
  7.2 1.0 slice.72
  8.2 0.9 convert_multiply_fusion.1
  9.2 0.7 mul.136
  9.9 0.1 square.24
  10.0 0.2 reduce_sum.88
  10.2 0.2 div.100
  10.4 0.1 div.101
  10.5 0.9 fusion.59
  11.4 0.7 pad_maximum_fusion.1
  12.2 0.1 add_reduce_fusion
  12.3 0.2 convert_reduce_fusion
  12.6 0.5 fusion.28
  13.1 9.8 %fusion.10 = bf16[2,128,3840]{2,1,0:T(8,128)(2,1)S(1)} fusion(bf16[2432,3840]{1,0:T(8,128)(2,1)} %param.18, bf16[1,2,128,2432]{3,2,1,0:T(8,128)(2,1)S(1)} %copy-done.1, f32[2432]{0:T(1024)S(1)} %get-tuple-element.39, f32[2432]{0:T(1024)S(1)} %get-tuple-element.40, f32[2,128]{1,0:T(2,128)S(1)} %add_sqrt_fusion.4, f32[2,128]{1,0:T(2,128)S(1)} %broadcast_multiply_fusion.1), kind=kOutput, calls=%fused_computation.15 | convolution fusion | flops 4786225152 | bytes 21910528 | tf_op jit(solution)/shard_map/kvx,xh->kvh/dot_general | solution.py:106
  22.9 1.3 copy-done.2
  24.2 1.2 convert_multiply_fusion
  25.4 1.7 copy.35
  27.1 0.1 reduce_sum.89
  27.2 1.2 div.104
  28.4 1.7 copy.36
  30.1 2.6 slice_convert_fusion
  32.7 1.3 fusion.48
  34.0 1.1 pad_maximum_fusion
  35.1 3.1 collective-permute-start
  38.9 1.7 copy.32
  40.6 0.2 multiply_reduce_fusion.2
  41.5 18.0 %all-gather.3.cloned.1.call-done = bf16[2,256,2560]{2,1,0:T(8,128)(2,1)} async-done(((bf16[2,16,2560]{2,1,0:T(8,128)(2,1)}), bf16[2,256,2560]{2,1,0:T(8,128)(2,1)}) %all-gather.3.cloned.1.call-update) | async-done | bytes 2621456 | tf_op jit(solution)/shard_map/all_gather | solution.py:123
  59.5 3.4 %fusion.79 = (bf16[2,256,1280]{2,1,0:T(8,128)(2,1)}, bf16[2,256,1280]{2,1,0:T(8,128)(2,1)}) fusion(bf16[2,256,2560]{2,1,0:T(8,128)(2,1)} %all-gather.3.cloned.1.call-done), kind=kLoop, calls=%fused_computation.98 | loop fusion | bytes 5242880 | tf_op jit(solution)/shard_map/slice | solution.py:59
  63.0 2.4 copy.33
  65.4 2.4 copy.34
  67.8 4.8 %fusion.13 = (f32[2,20,128]{2,1,0:T(8,128)S(1)}, f32[2,20,128,256]{3,2,1,0:T(8,128)}) fusion(pred[2,256]{1,0:T(4,128)(4,1)S(1)} %iota_compare_fusion, bf16[2,256,20,64]{1,3,2,0:T(8,128)(2,1)} %bitcast.118, f32[2,128,20,64]{1,3,2,0:T(8,128)S(1)} %bitcast.111, f32[64]{0:T(128)S(1)} %copy-done.6, f32[2,128,20]{1,2,0:T(8,128)S(1)} %add_sqrt_fusion.1), kind=kOutput, calls=%fused_computation.16 | convolution fusion | flops 172682240 | bytes 7906048 | tf_op jit(solution)/shard_map/bqhd,bkhd->bhqk/dot_general | solution.py:61
  72.7 122.5 %all-gather.5.cloned.1.call-done = bf16[2,2048,2560]{2,1,0:T(8,128)(2,1)} async-done(((bf16[2,128,2560]{2,1,0:T(8,128)(2,1)}), bf16[2,2048,2560]{2,1,0:T(8,128)(2,1)}) %all-gather.5.cloned.1.call-update) | async-done | bytes 20971536 | tf_op jit(solution)/shard_map/all_gather | solution.py:126
  195.2 15.9 %fusion.78 = (bf16[2,2048,1280]{2,1,0:T(8,128)(2,1)}, bf16[2,2048,1280]{2,1,0:T(8,128)(2,1)}) fusion(bf16[2,2048,2560]{2,1,0:T(8,128)(2,1)} %all-gather.5.cloned.1.call-done), kind=kLoop, calls=%fused_computation.97 | loop fusion | bytes 41943040 | tf_op jit(solution)/shard_map/slice | solution.py:58
  211.1 14.4 %copy.38 = bf16[2,2048,1280]{1,2,0:T(8,128)(2,1)} copy(bf16[2,2048,1280]{2,1,0:T(8,128)(2,1)} %get-tuple-element.56) | data formatting | bytes 20971520 | tf_op jit(solution)/shard_map/slice | solution.py:59
  225.5 14.4 %copy.37 = bf16[2,2048,1280]{1,2,0:T(8,128)(2,1)} copy(bf16[2,2048,1280]{2,1,0:T(8,128)(2,1)} %get-tuple-element.55) | data formatting | bytes 20971520 | tf_op jit(solution)/shard_map/slice | solution.py:58
  239.9 18.7 %multiply_reduce_fusion = (f32[2,20,128]{2,1,0:T(8,128)S(1)}, f32[2,20,128,2048]{3,2,1,0:T(8,128)}) fusion(bf16[2,2048,20,64]{1,3,2,0:T(8,128)(2,1)} %bitcast.109, f32[2,128,20,64]{1,3,2,0:T(8,128)S(1)} %bitcast.112, f32[64]{0:T(128)S(1)} %copy-done.6, f32[2,128,20]{1,2,0:T(8,128)S(1)} %add_sqrt_fusion.1), kind=kOutput, calls=%fused_computation.3 | convolution fusion | flops 1364126720 | bytes 53780736 | tf_op jit(solution)/shard_map/bqhd,bkhd->bhqk/dot_general | solution.py:61
  258.6 17.2 %fusion = f32[2,20,128]{2,1,0:T(8,128)S(1)} fusion(f32[2,20,128,2048]{3,2,1,0:T(8,128)} %get-tuple-element.67, f32[2,20,128]{2,1,0:T(8,128)S(1)} %get-tuple-element.63), kind=kLoop, calls=%fused_computation.4 | loop fusion | flops 31452160 | bytes 41984000 | tf_op jit(solution)/shard_map/reduce_sum | solution.py:69
  275.8 18.9 %fusion.35 = f32[2,128,20,64]{1,3,2,0:T(8,128)S(1)} fusion(bf16[2,2048,20,64]{1,3,2,0:T(8,128)(2,1)} %bitcast.108, f32[2,20,128,2048]{3,2,1,0:T(8,128)} %get-tuple-element.67, f32[2,20,128]{2,1,0:T(8,128)S(1)} %get-tuple-element.63), kind=kOutput, calls=%fused_computation.37 | convolution fusion | flops 1373634560 | bytes 53760000 | tf_op jit(solution)/shard_map/bhqk,bkhd->bhqd/dot_general | solution.py:70
  294.8 3.8 %fusion.20 = f32[2,20,128]{2,1,0:T(8,128)S(1)} fusion(f32[2,20,128,256]{3,2,1,0:T(8,128)} %get-tuple-element.65, f32[2,20,128]{2,1,0:T(8,128)S(1)} %get-tuple-element.62, pred[2,256]{1,0:T(4,128)(4,1)S(1)} %iota_compare_fusion), kind=kLoop, calls=%fused_computation.19 | loop fusion | flops 6548480 | bytes 5284352 | tf_op jit(solution)/shard_map/reduce_sum | solution.py:69
  298.7 4.2 %divide_convert_fusion = bf16[2,128,20,64]{1,3,2,0:T(8,128)(2,1)S(1)} fusion(f32[2,128,20,64]{1,3,2,0:T(8,128)S(1)} %fusion.35, bf16[2,256,20,64]{1,3,2,0:T(8,128)(2,1)S(1)} %bitcast.117, f32[2,20,128,256]{3,2,1,0:T(8,128)} %get-tuple-element.65, f32[2,20,128]{2,1,0:T(8,128)S(1)} %get-tuple-element.62, pred[2,256]{1,0:T(4,128)(4,1)S(1)} %iota_compare_fusion, ...), kind=kOutput, calls=%fused_computation.44 | convolution fusion | flops 175964160 | bytes 8602112 | tf_op jit(solution)/shard_map/bhqk,bkhd->bhqd/dot_general | solution.py:70
  302.9 0.2 slice-done.1
  303.1 2.1 fusion.80
  305.2 0.4 multiply_reduce_fusion.1
  305.6 0.7 fusion.54
  306.3 0.6 multiply_convert_fusion.1
  306.9 13.2 %all_gather.12 = bf16[8,128,64]{1,2,0:T(8,128)(2,1)S(1)} all-gather(bf16[1,128,64]{1,2,0:T(8,128)(2,1)S(1)} %get-tuple-element.51), channel_id=1, replica_groups=mesh['tm'=8,'seq'=16] {'tm'}, dimensions={0}, use_global_device_ids=true | all-gather | bytes 147456 | tf_op jit(solution)/shard_map/all_gather | solution.py:25
  320.1 1.2 while.10
  320.2 0.1 copy.45
  321.4 0.6 fusion.65
  (57 shorter events, 1.3 us)
Async XLA Ops:
  7.2 298.4 %copy-start = (bf16[2432,64]{0,1:T(8,128)(2,1)S(1)}, bf16[2432,64]{0,1:T(8,128)(2,1)}, u32[]{:S(2)}) copy-start(bf16[2432,64]{0,1:T(8,128)(2,1)} %param.22) | copy-start | bytes 933892
  7.2 5.0 %copy-start.4 = (f32[1,5,2432]{2,0,1:T(1,128)S(1)}, f32[1,5,2432]{2,0,1:T(1,128)}, u32[]{:S(2)}) copy-start(f32[1,5,2432]{2,0,1:T(1,128)} %param.17) | copy-start | bytes 145924
  7.2 5.1 %copy-start.1 = (bf16[1,2,128,2432]{3,2,1,0:T(8,128)(2,1)S(1)}, bf16[1,2,128,2432]{3,2,1,0:T(8,128)(2,1)}, u32[]{:S(2)}) copy-start(bf16[1,2,128,2432]{3,2,1,0:T(8,128)(2,1)} %param.13) | copy-start | bytes 3735556
  7.2 52.3 %all-gather.3.cloned.1.call-start = ((), (), s32[]{:S(2)}) async-start(), calls=%async_computation | async-start | bytes 2785280 | tf_op jit(solution)/shard_map/all_gather | solution.py:123
  12.1 183.0 %all-gather.5.cloned.1.call-start = ((), (), s32[]{:S(2)}) async-start(), calls=%async_computation.1 | async-start | bytes 22282240 | tf_op jit(solution)/shard_map/all_gather | solution.py:126
  22.9 1.3 copy-start.2
  35.1 5.7 %copy-start.7 = (s32[2]{0:T(128)S(1)}, s32[2]{0:T(128)}, u32[]{:S(2)}) copy-start(s32[2]{0:T(128)} %param.15) | copy-start | bytes 28
  35.1 5.8 %collective-permute-start = (s32[1]{0:T(128)}, s32[1]{0:T(128)}, u32[]{:S(2)}, u32[]{:S(2)}) collective-permute-start(s32[1]{0:T(128)} %param.16), channel_id=1, source_target_pairs={{16,0},{32,16},{48,32},{64,48},{80,64},{96,80},{112,96},{17,1},{33... | collective-permute-start | bytes 20 | tf_op jit(solution)/shard_map/ppermute | solution.py:20
  63.0 4.9 %copy-start.6 = (f32[64]{0:T(128)S(1)}, f32[64]{0:T(128)}, u32[]{:S(2)}) copy-start(f32[64]{0:T(128)} %param.19) | copy-start | bytes 772
  294.8 3.9 %copy-start.3 = (bf16[2,256,1280]{1,2,0:T(8,128)(2,1)S(1)}, bf16[2,256,1280]{1,2,0:T(8,128)(2,1)}, u32[]{:S(2)}) copy-start(bf16[2,256,1280]{1,2,0:T(8,128)(2,1)} %copy.34) | copy-start | bytes 3932164
  298.7 4.2 %slice-start = ((s8[6225920]{0:T(1024)(128)(4,1)}), s8[4194304]{0:T(1024)(128)(4,1)S(1)}, s32[]{:S(2)}) async-start(s8[6225920]{0:T(1024)(128)(4,1)} %bitcast.113), calls=%async_computation.2 | async-start | bytes 8388608
  298.7 4.4 %slice-start.1 = ((s8[6225920]{0:T(1024)(128)(4,1)}), s8[2031616]{0:T(1024)(128)(4,1)S(1)}, s32[]{:S(2)}) async-start(s8[6225920]{0:T(1024)(128)(4,1)} %bitcast.113), calls=%async_computation.3 | async-start | bytes 4063232
  305.6 15.8 %copy-start.5 = (f32[128,64]{0,1:T(8,128)S(1)}, f32[128,64]{0,1:T(8,128)}, u32[]{:S(2)}) copy-start(f32[128,64]{0,1:T(8,128)} %param.23) | copy-start | bytes 98308
Sparse Core Ops, SparseCore 0:
  12.3 47.2 all-gather.2
  61.7 133.4 all-gather.4
where the time goes:
time: 330 us; the launch traced here: 329 us
  waiting for transfers between devices  141 us (43%)
  local copies, waits for them, and re-layouts  63.9 us (19%)
  matrix products  59.3 us (18%)
  other arithmetic  33 us (10%)
  between operations  15.7 us (5%)
  blocking collectives  13.2 us (4%)
    all_gather x1, waiting for transfers between devices, on_device(): key_rows = lax.all_gather(image_local, 'seq', axis=1, tiled=True)  123 us
    slice x3, local copies, waits for them, and re-layouts, attend(): key_part = key_rows[:, :, :inner].reshape(2, row_count, heads, head_size)  32.8 us
    dot_general x2, matrix products, attend(): jnp.einsum('bqhd,bkhd->bhqk', query, key_part, preferred_element_type=jnp...  23.5 us
    dot_general x2, matrix products, attend(): jnp.einsum('bhqk,bkhd->bhqd', expon.astype(jnp.bfloat16), value_part, pre...  23.2 us
    reduce_sum x2, other arithmetic, attend(): denominator = denominator * factor + jnp.sum(expon, axis=-1)  21 us
    slice x3, local copies, waits for them, and re-layouts, attend(): value_part = key_rows[:, :, inner:].reshape(2, row_count, heads, head_size)  20.3 us
    all_gather x1, waiting for transfers between devices, on_device(): text_all = lax.all_gather(text_local, 'seq', axis=1, tiled=True)  18 us
    all_gather x1, blocking collectives, carried_in(): gathered = lax.all_gather(value.astype(jnp.bfloat16), axis)  13.2 us
  transfers between devices with their start and end apart: 3, of which 2 were waited for; matrix products, arithmetic and copies ran while one was open for 11% of the time, Pallas kernels for 0%

commit v1 on v0

v1 whole, which is shorter than its diff:
```python
import math

import jax
import jax.numpy as jnp
from jax import lax
from jax.experimental import pallas as pl
from jax.experimental.pallas import tpu as pltpu
from jax.sharding import PartitionSpec as P

NSTEPS = 28
EPSILON = 1e-06
NEG_LARGE = -1e30
GUIDANCE = 3.5
TIME_SHIFT = 3.0
LOG2E = 1.4426950408889634

MESH = pl.DeviceIdType.MESH
BF = jnp.bfloat16
F32 = jnp.float32

D = 2432
NSEQ = 16
NTM = 8
ROWS = 128
TROWS = 16
KEYS = 2048
TKEYS = 256
QB = 512
KC = 256
NT = (((1,), (1,)), ((), ()))

T, KV5, Q5, QP, KVA, KVB, OP, O5 = range(8)


def sigma_of(index_values):
    fraction = 1.0 - index_values / NSTEPS
    return TIME_SHIFT * fraction / (1.0 + (TIME_SHIFT - 1.0) * fraction)


def normalized(x):
    center = jnp.mean(x, axis=-1, keepdims=True)
    x = x - center
    spread = jnp.mean(x * x, axis=-1, keepdims=True)
    return x * lax.rsqrt(spread + EPSILON)


def head_mean_matrix():
    row = lax.broadcasted_iota(jnp.int32, (256, 256), 0) // 64
    col = lax.broadcasted_iota(jnp.int32, (256, 256), 1) // 64
    return jnp.where(row == col, 1.0 / 64, 0.0).astype(BF)


def head_norm(x, gain, mean_matrix):
    square = x * x
    high = square.astype(BF)
    low = (square - high.astype(F32)).astype(BF)
    mean = jnp.dot(high, mean_matrix, preferred_element_type=F32)
    mean += jnp.dot(low, mean_matrix, preferred_element_type=F32)
    return x * lax.rsqrt(mean + EPSILON) * gain


def interleave(keys, values, low_lanes):
    swapped = pltpu.roll(values, 64, 1)
    return jnp.where(low_lanes, keys, swapped), jnp.where(low_lanes, swapped, keys)


def attend(query, image_kv, text_kv, bias, key_lanes):
    query = jnp.where(key_lanes[:1], query, BF(0))
    maxima = total = None
    for start in range(0, KEYS + TKEYS, KC):
        if start < KEYS:
            block = image_kv[start : start + KC, :]
        else:
            block = text_kv[...]
        scores = lax.dot_general(query, block, NT, preferred_element_type=F32)
        if start >= KEYS:
            scores = scores + bias
        largest = jnp.max(scores, axis=1, keepdims=True)
        ones_values = jnp.where(key_lanes, BF(1), block)
        if maxima is None:
            expon = jnp.exp2(scores - largest).astype(BF)
            total = jnp.dot(expon, ones_values, preferred_element_type=F32)
        else:
            largest = jnp.maximum(maxima, largest)
            expon = jnp.exp2(scores - largest).astype(BF)
            total = total * jnp.exp2(maxima - largest) + jnp.dot(
                expon, ones_values, preferred_element_type=F32
            )
        maxima = largest
    return total


def kernel(
    hidden_hbm, text_hbm, lengths, plan, mod_hbm, wqkv_hbm, qgain, kgain, wout_hbm, wlat_hbm, anchor,
    velocity, latents,
    hid, text, mod, wqkv, wout, wlat, normed, h2,
    s_t, s_kv5, s_q5, s_q, s_kva, s_kvb, s_o, s_o5, text_kv,
    r_t, r_kv5, r_q5, r_q, r_kva, r_kvb, r_o5, mixed, res_a,
    drift, r_drift, sig, r_sig, next_sig,
    load_sem, w_sem, send_sem, recv_sem, dsend_sem, drecv_sem, sig_sem,
):
    tm = lax.axis_index("tm")
    me = lax.axis_index("seq")

    def load(source, target, sem):
        return pltpu.make_async_copy(source, target, sem)

    def block_of(slot):
        return 4 if isinstance(slot, int) and slot == 0 else lax.rem(me // 4 + slot - 1, 4)

    def w_load(slot, third):
        column = third * 1280 + block_of(slot) * 256
        if not isinstance(column, int):
            column = pl.multiple_of(column, 256)
        return load(wqkv_hbm.at[:, pl.ds(column, 256)], wqkv.at[slot * 3 + third], w_sem.at[slot * 3 + third])

    hid_load = load(hidden_hbm, hid, load_sem.at[0])
    mod_load = load(mod_hbm, mod, load_sem.at[1])
    text_load = load(text_hbm, text, load_sem.at[2])
    wout_load = load(wout_hbm, wout, load_sem.at[3])
    wlat_load = load(wlat_hbm, wlat, load_sem.at[4])
    hid_load.start()
    mod_load.start()
    for third in range(3):
        w_load(0, third).start()
    text_load.start()
    for slot in range(1, 5):
        for third in range(3):
            w_load(slot, third).start()
    wout_load.start()
    wlat_load.start()

    barrier = pltpu.get_barrier_semaphore()

    def greet_seq(j, carry):
        pl.semaphore_signal(barrier, inc=1, device_id=(tm, lax.rem(me + j, NSEQ)), device_id_type=MESH)
        return carry

    def greet_tm(j, carry):
        pl.semaphore_signal(barrier, inc=1, device_id=(lax.rem(tm + j, NTM), me), device_id_type=MESH)
        return carry

    lax.fori_loop(1, NSEQ, greet_seq, 0)
    lax.fori_loop(1, NTM, greet_tm, 0)

    def source_of(kind, to):
        if kind == T:
            return s_t.at[to]
        if kind == KV5:
            return s_kv5.at[to // 2]
        if kind == Q5:
            return s_q5.at[(to // 4) * 2 + lax.rem(to, 2)]
        if kind == QP:
            return s_q.at[to]
        if kind == KVA:
            return s_kva.at[to]
        if kind == KVB:
            return s_kvb.at[to]
        if kind == OP:
            return s_o.at[pl.ds(pl.multiple_of(to * ROWS, ROWS), ROWS), :]
        return s_o5.at[pl.ds(pl.multiple_of(to * 64, 64), 64), :]

    def target_of(kind, frm):
        rows = pl.ds(pl.multiple_of(frm * ROWS, ROWS), ROWS)
        if kind == T:
            return r_t.at[:, pl.ds(pl.multiple_of(frm * TROWS, TROWS), TROWS), :]
        if kind == KV5:
            return r_kv5.at[rows, :]
        if kind == Q5:
            return r_q5.at[pl.ds(pl.multiple_of(frm * 64, 64), 64), :]
        if kind == QP:
            return r_q.at[rows, :]
        if kind == KVA:
            return r_kva.at[rows, :]
        if kind == KVB:
            return r_kvb.at[rows, :]
        if kind == OP:
            branch = lax.rem(frm // 2, 2)
            pair = 2 * (frm // 4) + lax.rem(frm, 2)
            return mixed.at[pair, pl.ds(pl.multiple_of(branch * ROWS, ROWS), ROWS), :]
        return r_o5.at[frm]

    def transfer(kind, to, frm):
        return pltpu.make_async_remote_copy(
            src_ref=source_of(kind, to),
            dst_ref=target_of(kind, frm),
            send_sem=send_sem.at[kind, to],
            recv_sem=recv_sem.at[kind, frm],
            device_id=(tm, to),
            device_id_type=MESH,
        )

    def send(kind, to):
        @pl.when(to != me)
        def _():
            transfer(kind, to, me).start()

        @pl.when(to == me)
        def _():
            target_of(kind, me)[...] = source_of(kind, me)[...]

    def receive_all(kind):
        def one(j, carry):
            frm = lax.rem(me + j, NSEQ)
            pltpu.make_async_remote_copy(
                src_ref=source_of(kind, frm),
                dst_ref=target_of(kind, frm),
                send_sem=send_sem.at[kind, frm],
                recv_sem=recv_sem.at[kind, frm],
                device_id=(tm, frm),
                device_id_type=MESH,
            ).wait_recv()
            return carry

        lax.fori_loop(1, NSEQ, one, 0)

    low_row = lax.broadcasted_iota(jnp.int32, (1, 128), 1) < 64
    mean_matrix = head_mean_matrix()
    qg = qgain[...] * (LOG2E / math.sqrt(64))
    qg = jnp.concatenate([qg] * 4, axis=1)
    kg = jnp.concatenate([kgain[...]] * 4, axis=1)

    sig[...] = sigma_of(jnp.full((8, 128), plan[0], jnp.int32).astype(F32))
    hid_load.wait()
    mod_load.wait()

    def first_norm(i, carry):
        rows = pl.ds(pl.multiple_of(i * 32, 32), 32)
        x = normalized(hid[rows, :].astype(F32))
        normed[rows, :] = (x * (1.0 + mod[1:2, :]) + mod[0:1, :]).astype(BF)
        return carry

    lax.fori_loop(0, 8, first_norm, 0)

    def project(slot):
        parts = []
        for third in range(3):
            w_load(slot, third).wait()
            part = jnp.dot(normed[...], wqkv[slot * 3 + third], preferred_element_type=F32)
            if third < 2:
                part = part.astype(BF).astype(F32)
                part = head_norm(part, qg if third == 0 else kg, mean_matrix)
            parts.append(part)
        return parts

    q, k, v = project(0)
    for b in range(2):
        for s in range(2):
            lanes = slice(128 * s, 128 * s + 128)
            rows = slice(ROWS * b, ROWS * b + ROWS)
            first, second = interleave(k[rows, lanes], v[rows, lanes], low_row)
            item = (b * 2 + s) * 2
            s_kv5[item] = first.astype(BF)
            s_kv5[item + 1] = second.astype(BF)
            for half in range(2):
                s_q5[item + half] = q[ROWS * b + 64 * half : ROWS * b + 64 * half + 64, lanes].astype(BF)

    pl.semaphore_wait(barrier, NSEQ - 1 + NTM - 1)

    def send_shared(j, carry):
        to = lax.rem(me + j, NSEQ)
        send(KV5, to)
        send(Q5, to)
        return carry

    lax.fori_loop(0, NSEQ, send_shared, 0)

    text_load.wait()
    for c in range(5):
        lanes = slice(256 * c, 256 * c + 256)
        tk = head_norm(text[:, lanes].astype(F32), kg, mean_matrix)
        tv = text[:, 1280 + 256 * c : 1280 + 256 * c + 256].astype(F32)
        for s in range(2):
            sub = slice(128 * s, 128 * s + 128)
            first, second = interleave(tk[:, sub], tv[:, sub], low_row)
            text_kv[4 * c + 2 * s] = first.astype(BF)
            text_kv[4 * c + 2 * s + 1] = second.astype(BF)
    for to in range(NSEQ):
        b, pair = (to // 2) % 2, 2 * (to // 4) + to % 2
        s_t[to, 0] = text_kv[2 * pair, TROWS * b : TROWS * b + TROWS]
        s_t[to, 1] = text_kv[2 * pair + 1, TROWS * b : TROWS * b + TROWS]
        b, head = to // 8, 16 + (to // 2) % 4
        s_t[to, 2] = text_kv[head, TROWS * b : TROWS * b + TROWS]

    def send_text(j, carry):
        send(T, lax.rem(me + j, NSEQ))
        return carry

    lax.fori_loop(0, NSEQ, send_text, 0)

    def sig_copy(to):
        return pltpu.make_async_remote_copy(
            src_ref=sig, dst_ref=r_sig, send_sem=sig_sem.at[0], recv_sem=sig_sem.at[1],
            device_id=(to, me), device_id_type=MESH,
        )

    @pl.when(tm > 0)
    def _():
        sig_copy(tm - 1).start()

    def whole(slot, carry):
        q, k, v = project(slot)
        block = block_of(slot)
        for b in range(2):
            for s in range(2):
                lanes = slice(128 * s, 128 * s + 128)
                rows = slice(ROWS * b, ROWS * b + ROWS)
                to = block * 4 + b * 2 + s
                first, second = interleave(k[rows, lanes], v[rows, lanes], low_row)
                s_q[to] = q[rows, lanes].astype(BF)
                s_kva[to] = first.astype(BF)
                s_kvb[to] = second.astype(BF)
        for part in range(4):
            to = block * 4 + lax.rem(part + me, 4)
            send(QP, to)
            send(KVA, to)
        return carry

    lax.fori_loop(1, 5, whole, 0)

    def send_second(j, carry):
        send(KVB, lax.rem((me // 4) * 4 + j + me, NSEQ))
        return carry

    lax.fori_loop(0, NSEQ, send_second, 0)

    def bias_of(branch):
        key = lax.broadcasted_iota(jnp.int32, (1, TKEYS), 1)
        return jnp.where(key < lengths[branch], 0.0, NEG_LARGE)

    receive_all(KV5)
    receive_all(Q5)
    receive_all(T)
    second_head = lax.rem(me // 2, 2)
    lane = lax.broadcasted_iota(jnp.int32, (KC, 128), 1)
    shared_lanes = (lane // 64) == second_head
    bias5 = bias_of(me // 8)

    def shared_block(i, carry):
        rows = pl.ds(pl.multiple_of(i * QB, QB), QB)
        res = attend(r_q5[rows, :], r_kv5, r_t.at[2], bias5, shared_lanes)
        out = pltpu.roll(res, 64, 1) / res
        s_o5[rows, :] = jnp.where(shared_lanes[:1], out, 0.0).astype(BF)
        for part in range(QB // 64):
            send(O5, i * (QB // 64) + part)
        return carry

    lax.fori_loop(0, 1024 // QB, shared_block, 0)

    receive_all(QP)
    receive_all(KVA)
    bias = bias_of(lax.rem(me // 2, 2))
    low_lanes = lane < 64

    def first_block(i, carry):
        rows = pl.ds(pl.multiple_of(i * QB, QB), QB)
        res_a[rows, :] = attend(r_q[rows, :], r_kva, r_t.at[0], bias, low_lanes)
        return carry

    lax.fori_loop(0, KEYS // QB, first_block, 0)

    receive_all(KVB)
    high_lanes = lane >= 64

    def second_block(j, carry):
        i = lax.rem(j + me // 4, KEYS // QB)
        rows = pl.ds(pl.multiple_of(i * QB, QB), QB)
        second = attend(r_q[rows, :], r_kvb, r_t.at[1], bias, high_lanes)
        first = res_a[rows, :]
        above = jnp.where(low_row, second, first)
        below = jnp.where(low_row, first, second)
        s_o[rows, :] = (pltpu.roll(above, 64, 1) / below).astype(BF)
        for part in range(QB // ROWS):
            send(OP, i * (QB // ROWS) + part)
        return carry

    lax.fori_loop(0, KEYS // QB, second_block, 0)

    receive_all(O5)
    for b in range(2):
        for s in range(2):
            for half in range(2):
                first = (b * 2 + s) * 4 + half
                mixed[8 + s, ROWS * b + 64 * half : ROWS * b + 64 * half + 64, :] = r_o5[first] + r_o5[first + 2]
    wout_load.wait()
    wlat_load.wait()
    receive_all(OP)

    gathered = jnp.concatenate([mixed[i] for i in range(10)], axis=1)
    for start in range(0, D, 512):
        stop = min(D, start + 512)
        out = jnp.dot(gathered, wout[:, start:stop], preferred_element_type=F32)
        h2[:, start:stop] = hid[:, start:stop].astype(F32) + mod[2:3, start:stop] * out

    def second_norm(i, carry):
        rows = pl.ds(pl.multiple_of(i * 32, 32), 32)
        x = normalized(h2[rows, :])
        normed[rows, :] = (x * (1.0 + mod[4:5, :]) + mod[3:4, :]).astype(BF)
        return carry

    lax.fori_loop(0, 8, second_norm, 0)
    branches = jnp.dot(normed[...], wlat[...], preferred_element_type=F32)
    guided = branches[:ROWS] + GUIDANCE * (branches[ROWS:] - branches[:ROWS])
    velocity[...] = guided

    @pl.when(tm < NTM - 1)
    def _():
        sig_copy(tm).wait_recv()
        next_sig[...] = r_sig[...]

    @pl.when(tm == NTM - 1)
    def _():
        next_sig[...] = jnp.zeros_like(next_sig)

    step = (next_sig[...] - sig[...])[0:1, 0:64]
    drift[...] = step * guided

    def drift_copy(to, frm):
        return pltpu.make_async_remote_copy(
            src_ref=drift, dst_ref=r_drift.at[frm], send_sem=dsend_sem.at[to], recv_sem=drecv_sem.at[frm],
            device_id=(to, me), device_id_type=MESH,
        )

    for to in range(1, NTM):
        @pl.when(to > tm)
        def _():
            drift_copy(to, tm).start()

    latents[...] = anchor[...] + drift[...]
    for frm in range(NTM - 1):
        @pl.when(frm < tm)
        def _():
            drift_copy(frm, frm).wait_recv()
            latents[...] += r_drift[frm]

    for to in range(1, NTM):
        @pl.when(to > tm)
        def _():
            drift_copy(to, tm).wait_send()

    @pl.when(tm > 0)
    def _():
        sig_copy(tm - 1).wait_send()

    for kind in range(8):
        def done(j, carry):
            transfer(kind, lax.rem(me + j, NSEQ), me).wait_send()
            return carry

        lax.fori_loop(1, NSEQ, done, 0)


def on_device(
    hidden, text_states, text_lengths, plan_index, modulation, query_key_value_weight, query_gain, key_gain,
    attention_output_weight, latent_output_weight, anchor,
):
    any_spec = pl.BlockSpec(memory_space=pl.ANY)
    vmem = pl.BlockSpec(memory_space=pltpu.VMEM)
    smem = pl.BlockSpec(memory_space=pltpu.SMEM)
    tile = lambda *lead: pltpu.VMEM(lead + (128, 128), BF)
    velocity, latents = pl.pallas_call(
        kernel,
        out_shape=[jax.ShapeDtypeStruct((ROWS, 64), F32)] * 2,
        in_specs=[any_spec, any_spec, smem, smem, any_spec, any_spec, vmem, vmem, any_spec, any_spec, vmem],
        out_specs=[vmem, vmem],
        scratch_shapes=[
            pltpu.VMEM((256, D), BF),
            pltpu.VMEM((32, 2560), BF),
            pltpu.VMEM((5, D), F32),
            pltpu.VMEM((15, D, 256), BF),
            pltpu.VMEM((1280, D), BF),
            pltpu.VMEM((D, 64), BF),
            pltpu.VMEM((256, D), BF),
            pltpu.VMEM((256, D), F32),
            pltpu.VMEM((16, 3, TROWS, 128), BF),
            tile(8),
            pltpu.VMEM((8, 64, 128), BF),
            tile(16),
            tile(16),
            tile(16),
            pltpu.VMEM((KEYS, 128), BF),
            pltpu.VMEM((1024, 128), BF),
            pltpu.VMEM((20, 32, 128), BF),
            pltpu.VMEM((3, TKEYS, 128), BF),
            pltpu.VMEM((KEYS, 128), BF),
            pltpu.VMEM((1024, 128), BF),
            pltpu.VMEM((KEYS, 128), BF),
            pltpu.VMEM((KEYS, 128), BF),
            pltpu.VMEM((KEYS, 128), BF),
            pltpu.VMEM((16, 64, 128), BF),
            pltpu.VMEM((10, 256, 128), BF),
            pltpu.VMEM((KEYS, 128), F32),
            pltpu.VMEM((ROWS, 64), F32),
            pltpu.VMEM((NTM, ROWS, 64), F32),
            pltpu.VMEM((8, 128), F32),
            pltpu.VMEM((8, 128), F32),
            pltpu.VMEM((8, 128), F32),
            pltpu.SemaphoreType.DMA((5,)),
            pltpu.SemaphoreType.DMA((15,)),
            pltpu.SemaphoreType.DMA((8, NSEQ)),
            pltpu.SemaphoreType.DMA((8, NSEQ)),
            pltpu.SemaphoreType.DMA((NTM,)),
            pltpu.SemaphoreType.DMA((NTM,)),
            pltpu.SemaphoreType.DMA((2,)),
        ],
        compiler_params=pltpu.CompilerParams(
            collective_id=0, has_side_effects=True, vmem_limit_bytes=58 * 2**20
        ),
        cost_estimate=pl.CostEstimate(flops=9_600_000_000, bytes_accessed=28_000_000, transcendentals=12_000_000),
    )(
        hidden.reshape(256, D),
        text_states.reshape(32, 2560),
        text_lengths,
        plan_index,
        modulation[0],
        query_key_value_weight,
        query_gain[None],
        key_gain[None],
        attention_output_weight,
        latent_output_weight,
        anchor,
    )
    return velocity[None], latents[None]


def solution(mesh):
    in_specs = (
        P("tm", None, "seq", None),
        P("tm", None, "seq", None),
        P(),
        P("tm"),
        P("tm", None, None),
        P(),
        P(),
        P(),
        P(),
        P(),
        P("seq", None),
    )
    out_specs = (P("tm", "seq", None), P("tm", "seq", None))
    return jax.shard_map(
        on_device, mesh=mesh, in_specs=in_specs, out_specs=out_specs, check_vma=False
    )
```

time: 330 us -> 85.9 us (0.26)
  waiting for transfers between devices: 141 us -> 0 us
  Pallas kernels: 0 us -> 75.9 us
  matrix products: 59.3 us -> 0 us
  local copies, waits for them, and re-layouts: 63.9 us -> 8.01 us
  other arithmetic: 33 us -> 0 us
  between operations: 15.7 us -> 1.29 us
  blocking collectives: 13.2 us -> 0 us
    all_gather x2 -> x0, waiting for transfers between devices: 141 us -> none  [the longest x1 123 us: on_device(): key_rows = lax.all_gather(image_local, 'seq', axis=1, tiled=True)]
    pallas_call x0 -> x1, Pallas kernels: none -> 75.9 us  [on_device(): pl.pallas_call(kernel, out_shape=[jax.ShapeDtypeStruct((ROWS, 64), F32)]...]
    dot_general x7 -> x0, matrix products: 59.3 us -> none  [the longest x2 23.5 us: attend(): jnp.einsum('bqhd,bkhd->bhqk', query, key_part, preferred_element_type=jnp...]
    slice x7 -> x0, local copies, waits for them, and re-layouts: 54 us -> none  [the longest x3 32.8 us: attend(): key_part = key_rows[:, :, :inner].reshape(2, row_count, heads, head_size)]
    reduce_sum x8 -> x0, other arithmetic: 22.6 us -> none  [the longest x2 21 us: attend(): denominator = denominator * factor + jnp.sum(expon, axis=-1)]
    all_gather x1 -> x0, blocking collectives: 13.2 us -> none  [carried_in(): gathered = lax.all_gather(value.astype(jnp.bfloat16), axis)]
    unnamed x20 -> x5, local copies, waits for them, and re-layouts: 1.49 us -> 8.01 us
  transfers between devices with their start and end apart: 3 -> 0, of which waited for: 2 -> 0; matrix products, arithmetic and copies ran while one was open for 11% -> 0% of each run, Pallas kernels for 0% -> 0%
where the time goes in v1:
time: 85.9 us; the launch traced here: 85.2 us
  Pallas kernels  75.9 us (88%)
  local copies, waits for them, and re-layouts  8.01 us (9%)
  between operations  1.29 us (2%)
    pallas_call x1, Pallas kernels, on_device(): pl.pallas_call(kernel, out_shape=[jax.ShapeDtypeStruct((ROWS, 64), F32)]...  75.9 us
    unnamed x5, local copies, waits for them, and re-layouts  8.01 us

profile of v1, /device:TPU:15, one launch (start us, length us, event | category | flops | bytes accessed | tf_op | source)
XLA Modules:
  0.0 85.2 jit_solution(6132526710914497030)
XLA Ops:
  1.3 1.5 %copy.14.anchor = f32[128,64]{1,0:T(8,128)} copy(f32[128,64]{0,1:T(8,128)} %param.21) | data formatting | bytes 65536 | tf_op args[10]
  2.8 1.4 %copy.19 = f32[1,5,2432]{2,1,0:T(8,128)} copy(f32[1,5,2432]{2,0,1:T(1,128)} %param.15) | data formatting | bytes 97280
  4.2 2.0 %copy.13.wlat_hbm = bf16[2432,64]{1,0:T(8,128)(2,1)} copy(bf16[2432,64]{0,1:T(8,128)(2,1)} %param.20) | data formatting | bytes 622592 | tf_op args[9]
  6.2 75.9 %shard_map.122 = (f32[128,64]{1,0:T(8,128)}, f32[128,64]{1,0:T(8,128)}) custom-call(bf16[256,2432]{1,0:T(8,128)(2,1)} %bitcast.12, bf16[32,2560]{1,0:T(8,128)(2,1)} %bitcast.13, s32[2]{0:T(128)} %lengths.1, s32[1]{0:T(128)S(6)} %copy.20.plan, f32[5,2432]{1,0:T(8,128)} %bitcast.9, bf16[2432,3840]{1,0:T(8,128)(2,1)} %wqkv_hbm.1, f32[1,64]{1,0:T(1,128)} %bitcast.14, ...), custom_call_target="tpu_custom_call" | custom-call | flops 9600000000 | bytes 28000000 | tf_op jit(solution)/shard_map/pallas_call | solution.py:461
  82.1 1.5 %copy.15 = f32[1,128,64]{1,2,0:T(8,128)} copy(f32[1,128,64]{2,1,0:T(8,128)} %bitcast.11) | data formatting | bytes 65536
  83.7 1.5 %copy.16 = f32[1,128,64]{1,2,0:T(8,128)} copy(f32[1,128,64]{2,1,0:T(8,128)} %bitcast.10) | data formatting | bytes 65536

commit v2 on v1

--- a/solution.py
+++ b/solution.py
@@ -29,6 +29,11 @@
 KC = 256
 NT = (((1,), (1,)), ((), ()))
 
+OTHERS = sorted(
+    ((dz, dy) for dz in range(4) for dy in range(4) if dz or dy),
+    key=lambda step: -(min(step[0], 4 - step[0]) + min(step[1], 4 - step[1])),
+)
+
 T, KV5, Q5, QP, KVA, KVB, OP, O5 = range(8)
 
 
@@ -45,8 +50,8 @@
 
 
 def head_mean_matrix():
-    row = lax.broadcasted_iota(jnp.int32, (256, 256), 0) // 64
-    col = lax.broadcasted_iota(jnp.int32, (256, 256), 1) // 64
+    row = lax.broadcasted_iota(jnp.int32, (256, 256), 0) >> 6
+    col = lax.broadcasted_iota(jnp.int32, (256, 256), 1) >> 6
     return jnp.where(row == col, 1.0 / 64, 0.0).astype(BF)
 
 
@@ -59,9 +64,17 @@
     return x * lax.rsqrt(mean + EPSILON) * gain
 
 
+def swap(x):
+    return pltpu.roll(x, 64, 1)
+
+
 def interleave(keys, values, low_lanes):
-    swapped = pltpu.roll(values, 64, 1)
+    swapped = swap(values)
     return jnp.where(low_lanes, keys, swapped), jnp.where(low_lanes, swapped, keys)
+
+
+def keys_first(keys, values, low_lanes):
+    return jnp.where(low_lanes, keys, swap(values)), jnp.where(low_lanes, swap(keys), values)
 
 
 def attend(query, image_kv, text_kv, bias, key_lanes):
@@ -90,9 +103,18 @@
     return total
 
 
+def guide(branches):
+    return branches[:, :ROWS] + GUIDANCE * (branches[:, ROWS:] - branches[:, :ROWS])
+
+
+def finish(branches, total, anchor, velocity, latents):
+    velocity[...] = guide(branches[...])
+    latents[...] = anchor[...] + total[...]
+
+
 def kernel(
-    hidden_hbm, text_hbm, lengths, plan, mod_hbm, wqkv_hbm, qgain, kgain, wout_hbm, wlat_hbm, anchor,
-    velocity, latents,
+    hidden_hbm, text_hbm, lengths, plan, mod_hbm, wqkv_hbm, qgain, kgain, wout_hbm, wlat_hbm,
+    branches_out, total,
     hid, text, mod, wqkv, wout, wlat, normed, h2,
     s_t, s_kv5, s_q5, s_q, s_kva, s_kvb, s_o, s_o5, text_kv,
     r_t, r_kv5, r_q5, r_q, r_kva, r_kvb, r_o5, mixed, res_a,
@@ -101,12 +123,42 @@
 ):
     tm = lax.axis_index("tm")
     me = lax.axis_index("seq")
+    my_z, my_y = me // 4, lax.rem(me, 4)
+
+    def owner(block, z):
+        return z * 4 + lax.rem(block + 4 - z, 4)
+
+    def pair_of(device):
+        z = device // 4
+        block = lax.rem(z + lax.rem(device, 4), 4)
+        return z // 2, 2 * block + lax.rem(z, 2)
+
+    odd = lax.rem(my_z + my_y + tm, 2)
+
+    def extra_owners():
+        for dz in (2, 1, 3, 0):
+            for far in (1, 0):
+                dy = 2 * far + lax.rem(dz + odd, 2)
+                yield lax.rem(my_z + dz, 4) * 4 + lax.rem(my_y + dy, 4)
+
+    def extra_item(device):
+        return (device // 4) * 2 + lax.rem(device, 4) // 2
+
+    def extra_owner(item):
+        z = item // 2
+        return z * 4 + 2 * (item % 2) + lax.rem(z + tm, 2)
+
+    def others():
+        for dz, dy in OTHERS:
+            yield lax.rem(my_z + dz, 4) * 4 + lax.rem(my_y + dy, 4)
 
     def load(source, target, sem):
         return pltpu.make_async_copy(source, target, sem)
 
     def block_of(slot):
-        return 4 if isinstance(slot, int) and slot == 0 else lax.rem(me // 4 + slot - 1, 4)
+        if isinstance(slot, int) and slot == 0:
+            return 4
+        return jnp.where(slot == 0, 4, lax.rem(my_z + my_y + slot + 1, 4))
 
     def w_load(slot, third):
         column = third * 1280 + block_of(slot) * 256
@@ -124,11 +176,6 @@
     for third in range(3):
         w_load(0, third).start()
     text_load.start()
-    for slot in range(1, 5):
-        for third in range(3):
-            w_load(slot, third).start()
-    wout_load.start()
-    wlat_load.start()
 
     barrier = pltpu.get_barrier_semaphore()
 
@@ -142,14 +189,19 @@
 
     lax.fori_loop(1, NSEQ, greet_seq, 0)
     lax.fori_loop(1, NTM, greet_tm, 0)
+
+    def query_rows(device):
+        z = device // 4
+        place = lax.rem(z + lax.rem(device, 4), 4) * 4 + z
+        return pl.ds(pl.multiple_of(place * ROWS, ROWS), ROWS)
 
     def source_of(kind, to):
         if kind == T:
             return s_t.at[to]
         if kind == KV5:
-            return s_kv5.at[to // 2]
+            return s_kv5.at[extra_item(to)]
         if kind == Q5:
-            return s_q5.at[(to // 4) * 2 + lax.rem(to, 2)]
+            return s_q5.at[extra_item(to)]
         if kind == QP:
             return s_q.at[to]
         if kind == KVA:
@@ -157,7 +209,7 @@
         if kind == KVB:
             return s_kvb.at[to]
         if kind == OP:
-            return s_o.at[pl.ds(pl.multiple_of(to * ROWS, ROWS), ROWS), :]
+            return s_o.at[query_rows(to), :]
         return s_o5.at[pl.ds(pl.multiple_of(to * 64, 64), 64), :]
 
     def target_of(kind, frm):
@@ -169,16 +221,15 @@
         if kind == Q5:
             return r_q5.at[pl.ds(pl.multiple_of(frm * 64, 64), 64), :]
         if kind == QP:
-            return r_q.at[rows, :]
+            return r_q.at[query_rows(frm), :]
         if kind == KVA:
             return r_kva.at[rows, :]
         if kind == KVB:
             return r_kvb.at[rows, :]
         if kind == OP:
-            branch = lax.rem(frm // 2, 2)
-            pair = 2 * (frm // 4) + lax.rem(frm, 2)
+            branch, pair = pair_of(frm)
             return mixed.at[pair, pl.ds(pl.multiple_of(branch * ROWS, ROWS), ROWS), :]
-        return r_o5.at[frm]
+        return r_o5.at[extra_item(frm)]
 
     def transfer(kind, to, frm):
         return pltpu.make_async_remote_copy(
@@ -190,6 +241,9 @@
             device_id_type=MESH,
         )
 
+    def keep(kind):
+        target_of(kind, me)[...] = source_of(kind, me)[...]
+
     def send(kind, to):
         @pl.when(to != me)
         def _():
@@ -197,7 +251,7 @@
 
         @pl.when(to == me)
         def _():
-            target_of(kind, me)[...] = source_of(kind, me)[...]
+            keep(kind)
 
     def receive_all(kind):
         def one(j, carry):
@@ -227,7 +281,7 @@
     def first_norm(i, carry):
         rows = pl.ds(pl.multiple_of(i * 32, 32), 32)
         x = normalized(hid[rows, :].astype(F32))
-        normed[rows, :] = (x * (1.0 + mod[1:2, :]) + mod[0:1, :]).astype(BF)
+        normed[rows, :] = (x * (1.0 + mod[1]) + mod[0]).astype(BF)
         return carry
 
     lax.fori_loop(0, 8, first_norm, 0)
@@ -236,6 +290,11 @@
         parts = []
         for third in range(3):
             w_load(slot, third).wait()
+
+            @pl.when(slot < 4)
+            def _():
+                w_load(slot + 1, third).start()
+
             part = jnp.dot(normed[...], wqkv[slot * 3 + third], preferred_element_type=F32)
             if third < 2:
                 part = part.astype(BF).astype(F32)
@@ -243,27 +302,25 @@
             parts.append(part)
         return parts
 
-    q, k, v = project(0)
+    q, k, v = project(jnp.int32(0))
     for b in range(2):
         for s in range(2):
             lanes = slice(128 * s, 128 * s + 128)
             rows = slice(ROWS * b, ROWS * b + ROWS)
-            first, second = interleave(k[rows, lanes], v[rows, lanes], low_row)
+            first, second = keys_first(k[rows, lanes], v[rows, lanes], low_row)
             item = (b * 2 + s) * 2
             s_kv5[item] = first.astype(BF)
             s_kv5[item + 1] = second.astype(BF)
-            for half in range(2):
-                s_q5[item + half] = q[ROWS * b + 64 * half : ROWS * b + 64 * half + 64, lanes].astype(BF)
+            above = q[ROWS * b : ROWS * b + 64, lanes]
+            below = q[ROWS * b + 64 : ROWS * b + ROWS, lanes]
+            s_q5[item] = jnp.where(low_row, above, swap(below)).astype(BF)
+            s_q5[item + 1] = jnp.where(low_row, swap(above), below).astype(BF)
 
     pl.semaphore_wait(barrier, NSEQ - 1 + NTM - 1)
 
-    def send_shared(j, carry):
-        to = lax.rem(me + j, NSEQ)
+    for to in extra_owners():
         send(KV5, to)
         send(Q5, to)
-        return carry
-
-    lax.fori_loop(0, NSEQ, send_shared, 0)
 
     text_load.wait()
     for c in range(5):
@@ -272,21 +329,21 @@
         tv = text[:, 1280 + 256 * c : 1280 + 256 * c + 256].astype(F32)
         for s in range(2):
             sub = slice(128 * s, 128 * s + 128)
-            first, second = interleave(tk[:, sub], tv[:, sub], low_row)
+            arrange = keys_first if c == 4 else interleave
+            first, second = arrange(tk[:, sub], tv[:, sub], low_row)
             text_kv[4 * c + 2 * s] = first.astype(BF)
             text_kv[4 * c + 2 * s + 1] = second.astype(BF)
     for to in range(NSEQ):
-        b, pair = (to // 2) % 2, 2 * (to // 4) + to % 2
+        b, pair = to // 8, 2 * ((to // 4 + to) % 4) + (to // 4) % 2
         s_t[to, 0] = text_kv[2 * pair, TROWS * b : TROWS * b + TROWS]
         s_t[to, 1] = text_kv[2 * pair + 1, TROWS * b : TROWS * b + TROWS]
-        b, head = to // 8, 16 + (to // 2) % 4
+        item = (to // 4) * 2 + (to % 4) // 2
+        b, head = item // 4, 16 + item % 4
         s_t[to, 2] = text_kv[head, TROWS * b : TROWS * b + TROWS]
 
-    def send_text(j, carry):
-        send(T, lax.rem(me + j, NSEQ))
-        return carry
-
-    lax.fori_loop(0, NSEQ, send_text, 0)
+    for to in others():
+        transfer(T, to, me).start()
+    keep(T)
 
     def sig_copy(to):
         return pltpu.make_async_remote_copy(
@@ -305,52 +362,56 @@
             for s in range(2):
                 lanes = slice(128 * s, 128 * s + 128)
                 rows = slice(ROWS * b, ROWS * b + ROWS)
-                to = block * 4 + b * 2 + s
+                to = owner(block, 2 * b + s)
                 first, second = interleave(k[rows, lanes], v[rows, lanes], low_row)
                 s_q[to] = q[rows, lanes].astype(BF)
                 s_kva[to] = first.astype(BF)
                 s_kvb[to] = second.astype(BF)
-        for part in range(4):
-            to = block * 4 + lax.rem(part + me, 4)
+        for dz in (2, 1, 3, 0):
+            to = owner(block, lax.rem(my_z + dz, 4))
             send(QP, to)
             send(KVA, to)
         return carry
 
     lax.fori_loop(1, 5, whole, 0)
-
-    def send_second(j, carry):
-        send(KVB, lax.rem((me // 4) * 4 + j + me, NSEQ))
-        return carry
-
-    lax.fori_loop(0, NSEQ, send_second, 0)
+    wout_load.start()
+    wlat_load.start()
+
+    for to in others():
+        transfer(KVB, to, me).start()
+    keep(KVB)
 
     def bias_of(branch):
         key = lax.broadcasted_iota(jnp.int32, (1, TKEYS), 1)
         return jnp.where(key < lengths[branch], 0.0, NEG_LARGE)
 
-    receive_all(KV5)
-    receive_all(Q5)
+    lane = lax.broadcasted_iota(jnp.int32, (KC, 128), 1)
+    low_lanes, high_lanes = lane < 64, lane >= 64
+    bias = bias_of(me // 8)
     receive_all(T)
-    second_head = lax.rem(me // 2, 2)
-    lane = lax.broadcasted_iota(jnp.int32, (KC, 128), 1)
-    shared_lanes = (lane // 64) == second_head
-    bias5 = bias_of(me // 8)
-
-    def shared_block(i, carry):
-        rows = pl.ds(pl.multiple_of(i * QB, QB), QB)
-        res = attend(r_q5[rows, :], r_kv5, r_t.at[2], bias5, shared_lanes)
-        out = pltpu.roll(res, 64, 1) / res
-        s_o5[rows, :] = jnp.where(shared_lanes[:1], out, 0.0).astype(BF)
-        for part in range(QB // 64):
-            send(O5, i * (QB // 64) + part)
-        return carry
-
-    lax.fori_loop(0, 1024 // QB, shared_block, 0)
+
+    @pl.when(odd == 0)
+    def _():
+        receive_all(KV5)
+        receive_all(Q5)
+
+        def extra_block(i, carry):
+            rows = pl.ds(pl.multiple_of(i * QB, QB), QB)
+            packed = r_q5[rows, :]
+            first = attend(packed, r_kv5, r_t.at[2], bias, low_lanes)
+            second = attend(swap(packed.astype(F32)).astype(BF), r_kv5, r_t.at[2], bias, low_lanes)
+            above = jnp.where(low_row, swap(first), second)
+            below = jnp.where(low_row, first, swap(second))
+            s_o5[rows, :] = (above / below).astype(BF)
+            return carry
+
+        lax.fori_loop(0, 1024 // QB, extra_block, 0)
+        for to in others():
+            transfer(O5, to, me).start()
+        keep(O5)
 
     receive_all(QP)
     receive_all(KVA)
-    bias = bias_of(lax.rem(me // 2, 2))
-    low_lanes = lane < 64
 
     def first_block(i, carry):
         rows = pl.ds(pl.multiple_of(i * QB, QB), QB)
@@ -360,28 +421,36 @@
     lax.fori_loop(0, KEYS // QB, first_block, 0)
 
     receive_all(KVB)
-    high_lanes = lane >= 64
 
     def second_block(j, carry):
-        i = lax.rem(j + me // 4, KEYS // QB)
+        i = lax.rem(j + my_z + my_y + 2, 4)
         rows = pl.ds(pl.multiple_of(i * QB, QB), QB)
         second = attend(r_q[rows, :], r_kvb, r_t.at[1], bias, high_lanes)
         first = res_a[rows, :]
         above = jnp.where(low_row, second, first)
         below = jnp.where(low_row, first, second)
-        s_o[rows, :] = (pltpu.roll(above, 64, 1) / below).astype(BF)
-        for part in range(QB // ROWS):
-            send(OP, i * (QB // ROWS) + part)
+        s_o[rows, :] = (swap(above) / below).astype(BF)
+        for dz in (2, 1, 3, 0):
+            send(OP, owner(i, lax.rem(my_z + dz, 4)))
         return carry
 
     lax.fori_loop(0, KEYS // QB, second_block, 0)
 
-    receive_all(O5)
+    for item in range(8):
+        frm = extra_owner(item)
+
+        @pl.when(frm != me)
+        def _():
+            transfer(O5, frm, frm).wait_recv()
+
     for b in range(2):
         for s in range(2):
-            for half in range(2):
-                first = (b * 2 + s) * 4 + half
-                mixed[8 + s, ROWS * b + 64 * half : ROWS * b + 64 * half + 64, :] = r_o5[first] + r_o5[first + 2]
+            item = (b * 2 + s) * 2
+            first = r_o5[item].astype(F32)
+            second = r_o5[item + 1].astype(F32)
+            start = ROWS * b
+            mixed[8 + s, start : start + 64, :] = jnp.where(low_row, first, swap(second)).astype(BF)
+            mixed[8 + s, start + 64 : start + ROWS, :] = jnp.where(low_row, swap(first), second).astype(BF)
     wout_load.wait()
     wlat_load.wait()
     receive_all(OP)
@@ -390,18 +459,18 @@
     for start in range(0, D, 512):
         stop = min(D, start + 512)
         out = jnp.dot(gathered, wout[:, start:stop], preferred_element_type=F32)
-        h2[:, start:stop] = hid[:, start:stop].astype(F32) + mod[2:3, start:stop] * out
+        h2[:, start:stop] = hid[:, start:stop].astype(F32) + mod[2, :, start:stop] * out
 
     def second_norm(i, carry):
         rows = pl.ds(pl.multiple_of(i * 32, 32), 32)
         x = normalized(h2[rows, :])
-        normed[rows, :] = (x * (1.0 + mod[4:5, :]) + mod[3:4, :]).astype(BF)
+        normed[rows, :] = (x * (1.0 + mod[4]) + mod[3]).astype(BF)
         return carry
 
     lax.fori_loop(0, 8, second_norm, 0)
-    branches = jnp.dot(normed[...], wlat[...], preferred_element_type=F32)
-    guided = branches[:ROWS] + GUIDANCE * (branches[ROWS:] - branches[:ROWS])
-    velocity[...] = guided
+    branches = lax.dot_general(wlat[...], normed[...], NT, preferred_element_type=F32)
+    guided = guide(branches)
+    branches_out[...] = branches
 
     @pl.when(tm < NTM - 1)
     def _():
@@ -412,7 +481,7 @@
     def _():
         next_sig[...] = jnp.zeros_like(next_sig)
 
-    step = (next_sig[...] - sig[...])[0:1, 0:64]
+    step = (next_sig[...] - sig[...])[0:1, :]
     drift[...] = step * guided
 
     def drift_copy(to, frm):
@@ -426,12 +495,12 @@
         def _():
             drift_copy(to, tm).start()
 
-    latents[...] = anchor[...] + drift[...]
+    total[...] = drift[...]
     for frm in range(NTM - 1):
         @pl.when(frm < tm)
         def _():
             drift_copy(frm, frm).wait_recv()
-            latents[...] += r_drift[frm]
+            total[...] += r_drift[frm]
 
     for to in range(1, NTM):
         @pl.when(to > tm)
@@ -442,9 +511,24 @@
     def _():
         sig_copy(tm - 1).wait_send()
 
-    for kind in range(8):
+    for kind in (T, QP, KVA, KVB, OP):
         def done(j, carry):
             transfer(kind, lax.rem(me + j, NSEQ), me).wait_send()
+            return carry
+
+        lax.fori_loop(1, NSEQ, done, 0)
+    for kind in (KV5, Q5):
+        for item in range(8):
+            to = extra_owner(item)
+
+            @pl.when(to != me)
+            def _():
+                transfer(kind, to, me).wait_send()
+
+    @pl.when(odd == 0)
+    def _():
+        def done(j, carry):
+            transfer(O5, lax.rem(me + j, NSEQ), me).wait_send()
             return carry
 
         lax.fori_loop(1, NSEQ, done, 0)
@@ -458,18 +542,18 @@
     vmem = pl.BlockSpec(memory_space=pltpu.VMEM)
     smem = pl.BlockSpec(memory_space=pltpu.SMEM)
     tile = lambda *lead: pltpu.VMEM(lead + (128, 128), BF)
-    velocity, latents = pl.pallas_call(
+    branches, total = pl.pallas_call(
         kernel,
-        out_shape=[jax.ShapeDtypeStruct((ROWS, 64), F32)] * 2,
-        in_specs=[any_spec, any_spec, smem, smem, any_spec, any_spec, vmem, vmem, any_spec, any_spec, vmem],
+        out_shape=[jax.ShapeDtypeStruct((64, 2 * ROWS), F32), jax.ShapeDtypeStruct((64, ROWS), F32)],
+        in_specs=[any_spec, any_spec, smem, smem, any_spec, any_spec, vmem, vmem, any_spec, any_spec],
         out_specs=[vmem, vmem],
         scratch_shapes=[
             pltpu.VMEM((256, D), BF),
             pltpu.VMEM((32, 2560), BF),
-            pltpu.VMEM((5, D), F32),
+            pltpu.VMEM((5, 1, D), F32),
             pltpu.VMEM((15, D, 256), BF),
             pltpu.VMEM((1280, D), BF),
-            pltpu.VMEM((D, 64), BF),
+            pltpu.VMEM((64, D), BF),
             pltpu.VMEM((256, D), BF),
             pltpu.VMEM((256, D), F32),
             pltpu.VMEM((16, 3, TROWS, 128), BF),
@@ -487,11 +571,11 @@
             pltpu.VMEM((KEYS, 128), BF),
             pltpu.VMEM((KEYS, 128), BF),
             pltpu.VMEM((KEYS, 128), BF),
-            pltpu.VMEM((16, 64, 128), BF),
+            pltpu.VMEM((8, 64, 128), BF),
             pltpu.VMEM((10, 256, 128), BF),
             pltpu.VMEM((KEYS, 128), F32),
-            pltpu.VMEM((ROWS, 64), F32),
-            pltpu.VMEM((NTM, ROWS, 64), F32),
+            pltpu.VMEM((64, ROWS), F32),
+            pltpu.VMEM((NTM, 64, ROWS), F32),
             pltpu.VMEM((8, 128), F32),
             pltpu.VMEM((8, 128), F32),
             pltpu.VMEM((8, 128), F32),
@@ -512,15 +596,20 @@
         text_states.reshape(32, 2560),
         text_lengths,
         plan_index,
-        modulation[0],
+        modulation.transpose(1, 0, 2),
         query_key_value_weight,
         query_gain[None],
         key_gain[None],
         attention_output_weight,
-        latent_output_weight,
-        anchor,
+        latent_output_weight.T,
     )
-    return velocity[None], latents[None]
+    velocity, latents = pl.pallas_call(
+        finish,
+        out_shape=[jax.ShapeDtypeStruct((64, ROWS), F32)] * 2,
+        in_specs=[vmem] * 3,
+        out_specs=[vmem] * 2,
+    )(branches, total, anchor.T)
+    return velocity.T[None], latents.T[None]
 
 
 def solution(mesh):

time: 85.9 us -> 71.2 us (0.83)
  local copies, waits for them, and re-layouts: 8.01 us -> 0 us
  Pallas kernels: 75.9 us -> 69.7 us
    unnamed x5 -> x0, local copies, waits for them, and re-layouts: 8.01 us -> none
    pallas_call x1 -> x2, Pallas kernels: 75.9 us -> 69.7 us  [the longest x1 68.2 us: on_device(): pl.pallas_call(kernel, out_shape=[jax.ShapeDtypeStruct((64, 2 * ROWS), F3...]
where the time goes in v2:
time: 71.2 us; the launch traced here: 71 us
  Pallas kernels  69.7 us (98%)
  between operations  1.29 us (2%)
    pallas_call x1, Pallas kernels, on_device(): pl.pallas_call(kernel, out_shape=[jax.ShapeDtypeStruct((64, 2 * ROWS), F3...  68.2 us
    pallas_call x1, Pallas kernels, on_device(): pl.pallas_call(finish, out_shape=[jax.ShapeDtypeStruct((64, ROWS), F32)]...  1.5 us

profile of v2, /device:TPU:15, one launch (start us, length us, event | category | flops | bytes accessed | tf_op | source)
XLA Modules:
  0.0 71.0 jit_solution(265012638037058000)
XLA Ops:
  1.3 68.2 %shard_map.122 = (f32[64,256]{1,0:T(8,128)}, f32[64,128]{1,0:T(8,128)}) custom-call(bf16[256,2432]{1,0:T(8,128)(2,1)} %bitcast.14, bf16[32,2560]{1,0:T(8,128)(2,1)} %bitcast.16, s32[2]{0:T(128)} %lengths.1, s32[1]{0:T(128)S(6)} %copy.13.plan, f32[5,1,2432]{2,1,0:T(1,128)} %bitcast.17, bf16[2432,3840]{1,0:T(8,128)(2,1)} %wqkv_hbm.1, f32[1,64]{1,0:T(1,128)} %bitcast.20, ...), custom_call_target="tpu_custom_call" | custom-call | flops 9600000000 | bytes 28000000 | tf_op jit(solution)/shard_map/pallas_call | solution.py:545
  69.5 1.5 %shard_map.123 = (f32[64,128]{1,0:T(8,128)}, f32[64,128]{1,0:T(8,128)}) custom-call(f32[64,256]{1,0:T(8,128)} %get-tuple-element.6.branches, f32[64,128]{1,0:T(8,128)} %get-tuple-element.7.total, f32[64,128]{1,0:T(8,128)} %bitcast.13), custom_call_target="tpu_custom_call" | custom-call | tf_op jit(solution)/shard_map/pallas_call | solution.py:606

commit v3 on v2

--- a/solution.py
+++ b/solution.py
@@ -25,7 +25,7 @@
 TROWS = 16
 KEYS = 2048
 TKEYS = 256
-QB = 512
+QB = 1024
 KC = 256
 NT = (((1,), (1,)), ((), ()))
 
@@ -117,7 +117,7 @@
     branches_out, total,
     hid, text, mod, wqkv, wout, wlat, normed, h2,
     s_t, s_kv5, s_q5, s_q, s_kva, s_kvb, s_o, s_o5, text_kv,
-    r_t, r_kv5, r_q5, r_q, r_kva, r_kvb, r_o5, mixed, res_a,
+    r_t, r_kv5, r_qx, r_q5, r_q, r_kva, r_kvb, r_o5, mixed, res_a,
     drift, r_drift, sig, r_sig, next_sig,
     load_sem, w_sem, send_sem, recv_sem, dsend_sem, drecv_sem, sig_sem,
 ):
@@ -171,11 +171,11 @@
     text_load = load(text_hbm, text, load_sem.at[2])
     wout_load = load(wout_hbm, wout, load_sem.at[3])
     wlat_load = load(wlat_hbm, wlat, load_sem.at[4])
+    text_load.start()
     hid_load.start()
     mod_load.start()
     for third in range(3):
         w_load(0, third).start()
-    text_load.start()
 
     barrier = pltpu.get_barrier_semaphore()
 
@@ -268,6 +268,31 @@
 
         lax.fori_loop(1, NSEQ, one, 0)
 
+    def sent_slot(slot):
+        for z in range(4):
+            to = owner(block_of(slot), z)
+
+            @pl.when(to != me)
+            def _():
+                transfer(QP, to, me).wait_send()
+                transfer(KVA, to, me).wait_send()
+
+    def sent_extra():
+        for kind in (KV5, Q5):
+            for item in range(8):
+                to = extra_owner(item)
+
+                @pl.when(to != me)
+                def _():
+                    transfer(kind, to, me).wait_send()
+
+    def sent_all(kind):
+        def one(j, carry):
+            transfer(kind, lax.rem(me + j, NSEQ), me).wait_send()
+            return carry
+
+        lax.fori_loop(1, NSEQ, one, 0)
+
     low_row = lax.broadcasted_iota(jnp.int32, (1, 128), 1) < 64
     mean_matrix = head_mean_matrix()
     qg = qgain[...] * (LOG2E / math.sqrt(64))
@@ -275,53 +300,6 @@
     kg = jnp.concatenate([kgain[...]] * 4, axis=1)
 
     sig[...] = sigma_of(jnp.full((8, 128), plan[0], jnp.int32).astype(F32))
-    hid_load.wait()
-    mod_load.wait()
-
-    def first_norm(i, carry):
-        rows = pl.ds(pl.multiple_of(i * 32, 32), 32)
-        x = normalized(hid[rows, :].astype(F32))
-        normed[rows, :] = (x * (1.0 + mod[1]) + mod[0]).astype(BF)
-        return carry
-
-    lax.fori_loop(0, 8, first_norm, 0)
-
-    def project(slot):
-        parts = []
-        for third in range(3):
-            w_load(slot, third).wait()
-
-            @pl.when(slot < 4)
-            def _():
-                w_load(slot + 1, third).start()
-
-            part = jnp.dot(normed[...], wqkv[slot * 3 + third], preferred_element_type=F32)
-            if third < 2:
-                part = part.astype(BF).astype(F32)
-                part = head_norm(part, qg if third == 0 else kg, mean_matrix)
-            parts.append(part)
-        return parts
-
-    q, k, v = project(jnp.int32(0))
-    for b in range(2):
-        for s in range(2):
-            lanes = slice(128 * s, 128 * s + 128)
-            rows = slice(ROWS * b, ROWS * b + ROWS)
-            first, second = keys_first(k[rows, lanes], v[rows, lanes], low_row)
-            item = (b * 2 + s) * 2
-            s_kv5[item] = first.astype(BF)
-            s_kv5[item + 1] = second.astype(BF)
-            above = q[ROWS * b : ROWS * b + 64, lanes]
-            below = q[ROWS * b + 64 : ROWS * b + ROWS, lanes]
-            s_q5[item] = jnp.where(low_row, above, swap(below)).astype(BF)
-            s_q5[item + 1] = jnp.where(low_row, swap(above), below).astype(BF)
-
-    pl.semaphore_wait(barrier, NSEQ - 1 + NTM - 1)
-
-    for to in extra_owners():
-        send(KV5, to)
-        send(Q5, to)
-
     text_load.wait()
     for c in range(5):
         lanes = slice(256 * c, 256 * c + 256)
@@ -341,9 +319,59 @@
         b, head = item // 4, 16 + item % 4
         s_t[to, 2] = text_kv[head, TROWS * b : TROWS * b + TROWS]
 
+    hid_load.wait()
+    mod_load.wait()
+
+    def first_norm(i, carry):
+        rows = pl.ds(pl.multiple_of(i * 32, 32), 32)
+        x = normalized(hid[rows, :].astype(F32))
+        normed[rows, :] = (x * (1.0 + mod[1]) + mod[0]).astype(BF)
+        return carry
+
+    lax.fori_loop(0, 8, first_norm, 0, unroll=4)
+
+    def project(slot):
+        parts = []
+        for third in range(3):
+            w_load(slot, third).wait()
+            if isinstance(slot, int):
+                for later in (1, 2):
+                    w_load(later, third).start()
+            part = jnp.dot(normed[...], wqkv[slot * 3 + third], preferred_element_type=F32)
+            if third < 2:
+                part = part.astype(BF).astype(F32)
+                part = head_norm(part, qg if third == 0 else kg, mean_matrix)
+            parts.append(part)
+        return parts
+
+    q, k, v = project(0)
+    for b in range(2):
+        for s in range(2):
+            lanes = slice(128 * s, 128 * s + 128)
+            rows = slice(ROWS * b, ROWS * b + ROWS)
+            first, second = keys_first(k[rows, lanes], v[rows, lanes], low_row)
+            item = (b * 2 + s) * 2
+            s_kv5[item] = first.astype(BF)
+            s_kv5[item + 1] = second.astype(BF)
+            above = q[ROWS * b : ROWS * b + 64, lanes]
+            below = q[ROWS * b + 64 : ROWS * b + ROWS, lanes]
+            s_q5[item] = jnp.where(low_row, above, swap(below)).astype(BF)
+            s_q5[item + 1] = jnp.where(low_row, swap(above), below).astype(BF)
+
+    for later in (3, 4):
+        for third in range(3):
+            w_load(later, third).start()
+    wout_load.start()
+    wlat_load.start()
+    pl.semaphore_wait(barrier, NSEQ - 1 + NTM - 1)
+
     for to in others():
         transfer(T, to, me).start()
     keep(T)
+    for to in extra_owners():
+        send(KV5, to)
+        send(Q5, to)
+
 
     def sig_copy(to):
         return pltpu.make_async_remote_copy(
@@ -367,6 +395,12 @@
                 s_q[to] = q[rows, lanes].astype(BF)
                 s_kva[to] = first.astype(BF)
                 s_kvb[to] = second.astype(BF)
+        @pl.when(slot == 1)
+        def _():
+            sent_extra()
+            sent_all(T)
+            receive_all(T)
+
         for dz in (2, 1, 3, 0):
             to = owner(block, lax.rem(my_z + dz, 4))
             send(QP, to)
@@ -374,12 +408,6 @@
         return carry
 
     lax.fori_loop(1, 5, whole, 0)
-    wout_load.start()
-    wlat_load.start()
-
-    for to in others():
-        transfer(KVB, to, me).start()
-    keep(KVB)
 
     def bias_of(branch):
         key = lax.broadcasted_iota(jnp.int32, (1, TKEYS), 1)
@@ -388,28 +416,36 @@
     lane = lax.broadcasted_iota(jnp.int32, (KC, 128), 1)
     low_lanes, high_lanes = lane < 64, lane >= 64
     bias = bias_of(me // 8)
-    receive_all(T)
-
     @pl.when(odd == 0)
     def _():
         receive_all(KV5)
         receive_all(Q5)
 
+        packed = r_q5[...]
+        unpacked = jnp.concatenate([packed, swap(packed.astype(F32)).astype(BF)], axis=0)
+
         def extra_block(i, carry):
-            rows = pl.ds(pl.multiple_of(i * QB, QB), QB)
-            packed = r_q5[rows, :]
-            first = attend(packed, r_kv5, r_t.at[2], bias, low_lanes)
-            second = attend(swap(packed.astype(F32)).astype(BF), r_kv5, r_t.at[2], bias, low_lanes)
-            above = jnp.where(low_row, swap(first), second)
-            below = jnp.where(low_row, first, swap(second))
-            s_o5[rows, :] = (above / below).astype(BF)
+            res_a[pl.ds(pl.multiple_of(i * QB, QB), QB), :] = attend(
+                r_qx[pl.ds(pl.multiple_of(i * QB, QB), QB), :], r_kv5, r_t.at[2], bias, low_lanes
+            )
             return carry
 
-        lax.fori_loop(0, 1024 // QB, extra_block, 0)
+        r_qx[...] = unpacked
+        lax.fori_loop(0, 2, extra_block, 0)
+        first, second = res_a[0:1024, :], res_a[1024:2048, :]
+        above = jnp.where(low_row, swap(first), second)
+        below = jnp.where(low_row, first, swap(second))
+        s_o5[...] = (above / below).astype(BF)
         for to in others():
             transfer(O5, to, me).start()
         keep(O5)
 
+    for slot in range(1, 4):
+        sent_slot(slot)
+    for to in others():
+        transfer(KVB, to, me).start()
+    keep(KVB)
+
     receive_all(QP)
     receive_all(KVA)
 
@@ -423,15 +459,16 @@
     receive_all(KVB)
 
     def second_block(j, carry):
-        i = lax.rem(j + my_z + my_y + 2, 4)
-        rows = pl.ds(pl.multiple_of(i * QB, QB), QB)
+        start = lax.rem(j + (my_z + my_y + 2) // 2, 2) * QB
+        rows = pl.ds(pl.multiple_of(start, QB), QB)
         second = attend(r_q[rows, :], r_kvb, r_t.at[1], bias, high_lanes)
         first = res_a[rows, :]
         above = jnp.where(low_row, second, first)
         below = jnp.where(low_row, first, second)
         s_o[rows, :] = (swap(above) / below).astype(BF)
-        for dz in (2, 1, 3, 0):
-            send(OP, owner(i, lax.rem(my_z + dz, 4)))
+        for part in range(2):
+            for dz in (2, 1, 3, 0):
+                send(OP, owner(start // 512 + part, lax.rem(my_z + dz, 4)))
         return carry
 
     lax.fori_loop(0, KEYS // QB, second_block, 0)
@@ -453,21 +490,39 @@
             mixed[8 + s, start + 64 : start + ROWS, :] = jnp.where(low_row, swap(first), second).astype(BF)
     wout_load.wait()
     wlat_load.wait()
-    receive_all(OP)
-
-    gathered = jnp.concatenate([mixed[i] for i in range(10)], axis=1)
-    for start in range(0, D, 512):
-        stop = min(D, start + 512)
-        out = jnp.dot(gathered, wout[:, start:stop], preferred_element_type=F32)
-        h2[:, start:stop] = hid[:, start:stop].astype(F32) + mod[2, :, start:stop] * out
+
+    def add_block(block, first):
+        pair = jnp.concatenate([mixed[2 * block], mixed[2 * block + 1]], axis=1)
+        depth = pl.ds(pl.multiple_of(block * 256, 256), 256)
+        for start in range(0, D, 512):
+            stop = min(D, start + 512)
+            out = jnp.dot(pair, wout[depth, start:stop], preferred_element_type=F32)
+            h2[:, start:stop] = out if first else h2[:, start:stop] + out
+
+    add_block(4, True)
+    my_class = lax.rem(my_z + my_y, 4)
+
+    def returned(k, carry):
+        block = 2 * lax.rem(my_class // 2 + 1 + k // 2, 2) + lax.rem(k, 2)
+        for z in range(4):
+            frm = owner(block, z)
+
+            @pl.when(frm != me)
+            def _():
+                transfer(OP, frm, frm).wait_recv()
+
+        add_block(block, False)
+        return carry
+
+    lax.fori_loop(0, 4, returned, 0)
 
     def second_norm(i, carry):
         rows = pl.ds(pl.multiple_of(i * 32, 32), 32)
-        x = normalized(h2[rows, :])
+        x = normalized(hid[rows, :].astype(F32) + mod[2] * h2[rows, :])
         normed[rows, :] = (x * (1.0 + mod[4]) + mod[3]).astype(BF)
         return carry
 
-    lax.fori_loop(0, 8, second_norm, 0)
+    lax.fori_loop(0, 8, second_norm, 0, unroll=4)
     branches = lax.dot_general(wlat[...], normed[...], NT, preferred_element_type=F32)
     guided = guide(branches)
     branches_out[...] = branches
@@ -511,27 +566,13 @@
     def _():
         sig_copy(tm - 1).wait_send()
 
-    for kind in (T, QP, KVA, KVB, OP):
-        def done(j, carry):
-            transfer(kind, lax.rem(me + j, NSEQ), me).wait_send()
-            return carry
-
-        lax.fori_loop(1, NSEQ, done, 0)
-    for kind in (KV5, Q5):
-        for item in range(8):
-            to = extra_owner(item)
-
-            @pl.when(to != me)
-            def _():
-                transfer(kind, to, me).wait_send()
-
+    for slot in range(4, 5):
+        sent_slot(slot)
+    for kind in (KVB, OP):
+        sent_all(kind)
     @pl.when(odd == 0)
     def _():
-        def done(j, carry):
-            transfer(O5, lax.rem(me + j, NSEQ), me).wait_send()
-            return carry
-
-        lax.fori_loop(1, NSEQ, done, 0)
+        sent_all(O5)
 
 
 def on_device(
@@ -566,6 +607,7 @@
             pltpu.VMEM((1024, 128), BF),
             pltpu.VMEM((20, 32, 128), BF),
             pltpu.VMEM((3, TKEYS, 128), BF),
+            pltpu.VMEM((KEYS, 128), BF),
             pltpu.VMEM((KEYS, 128), BF),
             pltpu.VMEM((1024, 128), BF),
             pltpu.VMEM((KEYS, 128), BF),

time: 71.2 us -> 64 us (0.90)
  Pallas kernels: 69.7 us -> 62 us
    pallas_call x1, Pallas kernels: 68.2 us -> 60.5 us  [on_device(): pl.pallas_call(kernel, out_shape=[jax.ShapeDtypeStruct((64, 2 * ROWS), F3...]
where the time goes in v3:
time: 64 us; the launch traced here: 63.3 us
  Pallas kernels  62 us (97%)
  between operations  1.29 us (2%)
    pallas_call x1, Pallas kernels, on_device(): pl.pallas_call(kernel, out_shape=[jax.ShapeDtypeStruct((64, 2 * ROWS), F3...  60.5 us
    pallas_call x1, Pallas kernels, on_device(): pl.pallas_call(finish, out_shape=[jax.ShapeDtypeStruct((64, ROWS), F32)]...  1.5 us

profile of v3, /device:TPU:15, one launch (start us, length us, event | category | flops | bytes accessed | tf_op | source)
XLA Modules:
  0.0 63.3 jit_solution(2644009918207779155)
XLA Ops:
  1.3 60.5 %shard_map.122 = (f32[64,256]{1,0:T(8,128)}, f32[64,128]{1,0:T(8,128)}) custom-call(bf16[256,2432]{1,0:T(8,128)(2,1)} %bitcast.14, bf16[32,2560]{1,0:T(8,128)(2,1)} %bitcast.16, s32[2]{0:T(128)} %lengths.1, s32[1]{0:T(128)S(6)} %copy.13.plan, f32[5,1,2432]{2,1,0:T(1,128)} %bitcast.17, bf16[2432,3840]{1,0:T(8,128)(2,1)} %wqkv_hbm.1, f32[1,64]{1,0:T(1,128)} %bitcast.20, ...), custom_call_target="tpu_custom_call" | custom-call | flops 9600000000 | bytes 28000000 | tf_op jit(solution)/shard_map/pallas_call | solution.py:586
  61.8 1.5 %shard_map.123 = (f32[64,128]{1,0:T(8,128)}, f32[64,128]{1,0:T(8,128)}) custom-call(f32[64,256]{1,0:T(8,128)} %get-tuple-element.6.branches, f32[64,128]{1,0:T(8,128)} %get-tuple-element.7.total, f32[64,128]{1,0:T(8,128)} %bitcast.13), custom_call_target="tpu_custom_call" | custom-call | tf_op jit(solution)/shard_map/pallas_call | solution.py:648
